TPU v7x, 256 devices: a whole 4x4x8 slice. The times are simulated.
256 devices in a mesh: row: 32 (over z, y), col: 8 (over x, core).
Axes of the slice: x: 4, y: 4, z: 8, core: 2. Of those that a mesh axis runs over, the one named last changes fastest.
Arguments:
- image: bfloat16 [16384, 512], P(('row', 'col')), may hold values from -2 to 2
- text: bfloat16 [16384, 512], P(('row', 'col')), may hold values from -3 to 3
- logit_scale: float32 [1], replicated, may hold values from 10 to 100
Outputs:
- loss: float32 [1], replicated
- grad_image: float32 [16384, 512], P(('row', 'col'))
- grad_text: float32 [16384, 512], P(('row', 'col'))
All inputs are finite; a program needn't handle non-finite values.
Results may differ from a plain program's by a relative error of at most 0.0095.
Values may be sent and summed in bfloat16 or wider, within the bound.
A program may use at most 64 MiB of HBM per device.

v0:
```python
import jax
import jax.numpy as jnp
from jax import lax
from jax.sharding import Mesh
from jax.sharding import PartitionSpec as P

COL = ("col_0", "col_1")
ROW = ("row_0", "row_1")
ROW_COL = ("row_0", "row_1", "col_0", "col_1")


def in_order(tiles, dim):
    tiles = jnp.moveaxis(tiles, 0, dim)
    dims = tiles.shape
    return tiles.reshape(*dims[:dim], dims[dim] * dims[dim + 1], *dims[dim + 2 :])


def from_everyone(value, axis):
    copies = jnp.broadcast_to(value, (lax.axis_size(axis), *value.shape))
    return lax.all_to_all(copies, axis, split_axis=0, concat_axis=0, tiled=True)


def gathered_copies(value, axis, dim):
    return in_order(from_everyone(value, axis), dim)


def gather_axes(value, axes, dim):
    for axis in reversed(axes):
        value = lax.all_gather(value, axis, axis=dim, tiled=True)
    return value


def all_in_one(value, axis):
    leaves = jax.tree.leaves(value)
    turns = sorted(range(len(leaves)), key=lambda k: -leaves[k].size)
    width = (1, *leaves[turns[0]].shape)[-1]
    lines = [
        jnp.pad(leaves[k].reshape(-1), (0, -leaves[k].size % width)).reshape(-1, width)
        for k in turns
    ]
    both, at, found = (from_everyone(jnp.concatenate(lines), axis), 0, {})
    for k, line in zip(turns, lines):
        share = both[:, at : at + len(line)].reshape(len(both), -1)
        found[k] = share[:, : leaves[k].size].reshape(-1, *leaves[k].shape)
        at += len(line)
    numbers = iter(range(len(leaves)))
    return jax.tree.map(lambda _: found[next(numbers)], value)


def joined_by_halves(pieces, combine):
    while len(jax.tree.leaves(pieces)[0]) > 1:
        pieces = jax.vmap(combine)(
            *(jax.tree.map(lambda part: part[side::2], pieces) for side in (0, 1))
        )
    return jax.tree.map(lambda part: part[0], pieces)


def combined_all(value, axis, combine):
    pieces = all_in_one(value, axis)
    return joined_by_halves(pieces, combine)


def all_in_one_2(value, axis):
    leaves = jax.tree.leaves(value)
    turns = sorted(range(len(leaves)), key=lambda k: -leaves[k].size)
    width = (1, *leaves[turns[0]].shape)[-1]
    lines = [
        jnp.pad(leaves[k].reshape(-1), (0, -leaves[k].size % width)).reshape(-1, width)
        for k in turns
    ]
    both, at, found = (lax.all_gather(jnp.concatenate(lines), axis), 0, {})
    for k, line in zip(turns, lines):
        share = both[:, at : at + len(line)].reshape(len(both), -1)
        found[k] = share[:, : leaves[k].size].reshape(-1, *leaves[k].shape)
        at += len(line)
    numbers = iter(range(len(leaves)))
    return jax.tree.map(lambda _: found[next(numbers)], value)


def merged_by_axis(value, axes, combine):
    for axis in axes:
        pieces = all_in_one_2(value, axis)
        value = jax.tree.map(lambda part: part[0], pieces)
        for k in range(1, lax.axis_size(axis)):
            value = combine(value, jax.tree.map(lambda part: part[k], pieces))
    return value


def over_axes(value, axes):
    for axis in axes:
        value = lax.psum(value, axis)
    return value


def sum_by_axis(total, axes):
    for axis in axes:
        total = lax.psum_scatter(total, axis, scatter_dimension=0, tiled=True)
    return total


def in_blocks(value, dim, count):
    dims = value.shape
    tiles = value.reshape(*dims[:dim], count, dims[dim] // count, *dims[dim + 1 :])
    return jnp.moveaxis(tiles, dim, 0)


def summed_on_arrival(value, axis, dim):
    count = lax.axis_size(axis)
    tiles = lax.all_to_all(in_blocks(value, dim, count), axis, 0, 0, tiled=True)
    return jnp.sum(tiles, axis=0)


def normalize(embedding):
    values = embedding.astype(jnp.float32)
    length = jnp.sqrt(jnp.sum(values * values, axis=1, keepdims=True) + 1e-06)
    return (values / length, length)


def unnormalize(unit_rows, length, gradient):
    return (gradient - unit_rows * jnp.sum(unit_rows * gradient, axis=1, keepdims=True)) / length


def combine(former, latter):
    summit = jnp.maximum(former[0], latter[0])
    return (
        summit,
        former[1] * jnp.exp(former[0] - summit) + latter[1] * jnp.exp(latter[0] - summit),
    )


def on_device(image, text, logit_scale):
    sharpness = logit_scale[0]
    unit_image, image_len = normalize(image)
    unit_text, text_len = normalize(text)
    img_own = unit_image.astype(jnp.bfloat16)
    txt_own = unit_text.astype(jnp.bfloat16)
    img_tile = gathered_copies(img_own, COL, 0)
    txt_tile = gather_axes(txt_own, ROW, 0)
    columns = txt_tile.shape[0]
    block_cols = min(512, columns)
    block_count = columns // block_cols
    txt_blocks = txt_tile.reshape(block_count, block_cols, txt_tile.shape[1])

    def scores(txt_block):
        return sharpness * jnp.einsum(
            "re,ce->rc", img_tile, txt_block, preferred_element_type=jnp.float32
        )

    lowest = jnp.full((img_tile.shape[0],), -1e30, jnp.float32)

    def online(running, txt_block):
        row_peak, row_sum = running
        logits = scores(txt_block)
        col_peak = jnp.max(logits, axis=0)
        col_sum = jnp.sum(jnp.exp(logits - col_peak[None, :]), axis=0)
        higher = jnp.maximum(row_peak, jnp.max(logits, axis=1))
        row_sum = row_sum * jnp.exp(row_peak - higher) + jnp.sum(
            jnp.exp(logits - higher[:, None]), axis=1
        )
        return ((higher, row_sum), (col_peak, col_sum))

    (row_peak, row_sum), (col_peak, col_sum) = lax.scan(
        online, (lowest, jnp.zeros_like(lowest)), txt_blocks
    )
    row_peak, row_sum = combined_all((row_peak, row_sum), COL, combine)
    col_peak, col_sum = merged_by_axis((col_peak.reshape(-1), col_sum.reshape(-1)), ROW, combine)
    row_lse = row_peak + jnp.log(row_sum)
    col_lse = col_peak + jnp.log(col_sum)
    own_rows = image.shape[0]
    row_mine = lax.dynamic_slice_in_dim(row_lse, lax.axis_index(COL) * own_rows, own_rows)
    col_mine = lax.dynamic_slice_in_dim(col_lse, lax.axis_index(ROW) * own_rows, own_rows)
    img_wide = img_own.astype(jnp.float32)
    txt_wide = txt_own.astype(jnp.float32)
    positive = sharpness * jnp.sum(img_wide * txt_wide, axis=1)
    partial_value = jnp.sum(row_mine - positive) + jnp.sum(col_mine - positive)
    overall = over_axes(partial_value, ROW_COL)
    batch_size = own_rows * lax.axis_size(ROW) * lax.axis_size(COL)
    loss = (overall / (2 * batch_size)).reshape(1)

    def weights_of(txt_block, lse_cols):
        logits = scores(txt_block)
        return (
            0.5 * (jnp.exp(logits - row_lse[:, None]) + jnp.exp(logits - lse_cols[None, :]))
        ).astype(jnp.bfloat16)

    start_grad = jnp.zeros((img_tile.shape[0], img_tile.shape[1]), jnp.float32)
    lse_blocks = col_lse.reshape(block_count, block_cols)

    def keep_weights(running, inputs):
        txt_block, lse_cols = inputs
        weights = weights_of(txt_block, lse_cols)
        running = running + sharpness * jnp.dot(
            weights, txt_block, preferred_element_type=jnp.float32
        )
        return (running, weights)

    img_terms, stored = lax.scan(keep_weights, start_grad, (txt_blocks, lse_blocks))
    flipped = jnp.swapaxes(stored, 1, 2).reshape(columns, img_tile.shape[0])
    txt_grad = sum_by_axis(
        sharpness * jnp.dot(flipped, img_tile, preferred_element_type=jnp.float32), ROW
    )
    img_grad = summed_on_arrival(img_terms, COL, 0)
    img_grad = img_grad - sharpness * txt_wide
    txt_grad = txt_grad - sharpness * img_wide
    return (
        loss,
        unnormalize(unit_image, image_len, img_grad),
        unnormalize(unit_text, text_len, txt_grad),
    )


def solution(mesh):
    torus = Mesh(mesh.devices.reshape(8, 4, 4, 2), ("row_0", "row_1", "col_0", "col_1"))
    return jax.shard_map(
        on_device,
        mesh=torus,
        in_specs=(P(ROW_COL, None), P(ROW_COL, None), P()),
        out_specs=(P(), P(ROW_COL, None), P(ROW_COL, None)),
        check_vma=False,
    )
```

profile of v0, /device:TPU:1, one launch (start us, length us, event | category | flops | bytes accessed | tf_op | source)
XLA Modules:
  0.0 286.2 jit_solution(1497360225404504215)
XLA Ops:
  7.2 1.0 fusion.11
  8.2 0.9 fusion.58
  9.1 11.9 %all_gather.18 = bf16[256,512]{1,0:T(8,128)(2,1)} all-gather(bf16[64,512]{1,0:T(8,128)(2,1)S(1)} %fusion.58), channel_id=1, replica_groups=mesh['row_0'=8,'row_1'=4,'col_0'=4,'col_1'=2] {'row_1'}, dimensions={0}, use_global_device_ids=true | all-gather | bytes 327680 | tf_op jit(solution)/shard_map/all_gather | solution.py:29
  21.1 1.0 fusion.12
  22.0 0.9 fusion.59
  23.0 0.8 broadcast_in_dim.39
  23.8 8.4 %all-to-all-start = ((bf16[8,64,512]{2,1,0:T(8,128)(2,1)}), bf16[8,64,512]{2,1,0:T(8,128)(2,1)}, u32[]{:S(2)}, u32[]{:S(2)}) async-start(bf16[8,64,512]{2,1,0:T(8,128)(2,1)} %broadcast_in_dim.39), calls=%async_computation | async-start | bytes 1048576 | tf_op jit(solution)/shard_map/all_to_all | solution.py:20
  32.8 8.9 %all-to-all-done = bf16[8,64,512]{2,1,0:T(8,128)(2,1)} async-done(((bf16[8,64,512]{2,1,0:T(8,128)(2,1)}), bf16[8,64,512]{2,1,0:T(8,128)(2,1)}, u32[]{:S(2)}, u32[]{:S(2)}) %all-to-all-start) | async-done | bytes 524320 | tf_op jit(solution)/shard_map/all_to_all | solution.py:20
  41.8 21.7 %all-gather.6.cloned.1.call-done = bf16[2048,512]{1,0:T(8,128)(2,1)} async-done(((bf16[256,512]{1,0:T(8,128)(2,1)}), bf16[2048,512]{1,0:T(8,128)(2,1)}) %all-gather.6.cloned.1.call-update) | async-done | bytes 2097168 | tf_op jit(solution)/shard_map/all_gather | solution.py:29
  63.5 11.7 %while.30 = (s32[]{:T(128)}, f32[512]{0:T(512)S(1)}, f32[512]{0:T(512)S(1)}, f32[4,512]{1,0:T(4,128)S(1)}, f32[4,512]{1,0:T(4,128)S(1)}, /*index=5*/f32[]{:T(128...) while((s32[]{:T(128)}, f32[512]{0:T(512)S(1)}, ...), condition=%wide.region_7.8_spmd.clone, body=%wide.region_2.7_spmd.clone.sunk | while | flops 270272000 | bytes 3187832 | solution.py:162
  63.5 2.4 fusion.77
  65.9 0.4 exponential_reduce_fusion.3
  66.3 0.1 dynamic_update_slice.18
  66.4 2.4 fusion.77
  68.8 0.4 exponential_reduce_fusion.3
  69.4 2.4 fusion.77
  71.8 0.4 exponential_reduce_fusion.3
  72.3 2.4 fusion.77
  74.7 0.4 exponential_reduce_fusion.3
  75.3 18.5 %all-gather.2 = f32[8,2,2048]{2,1,0:T(2,128)S(1)} all-gather(f32[1,2,2048]{2,1,0:T(2,128)S(1)} %maximum_bitcast_fusion), channel_id=2, replica_groups=mesh['row_0'=8,'row_1'=4,'col_0'=4,'col_1'=2] {'row_0'}, dimensions={0}, use_global_device_ids=true | all-gather | bytes 147456 | tf_op jit(solution)/shard_map/all_gather | solution.py:71
  93.8 0.2 fusion.17
  94.0 9.4 %all-gather.3 = f32[4,2,2048]{2,1,0:T(2,128)S(1)} all-gather(f32[1,2,2048]{2,1,0:T(2,128)S(1)} %maximum_bitcast_fusion.1), channel_id=3, replica_groups=mesh['row_0'=8,'row_1'=4,'col_0'=4,'col_1'=2] {'row_1'}, dimensions={0}, use_global_device_ids=true | all-gather | bytes 81920 | tf_op jit(solution)/shard_map/all_gather | solution.py:71
  103.4 0.2 slice_reduce_fusion.3
  103.7 0.6 broadcast_in_dim.40
  104.3 17.5 %all-to-all-start.1 = ((f32[8,2,512]{2,1,0:T(2,128)}), f32[8,2,512]{2,1,0:T(2,128)S(1)}, u32[]{:S(2)}, u32[]{:S(2)}) async-start(f32[8,2,512]{2,1,0:T(2,128)} %broadcast_in_dim.40), calls=%async_computation.1 | async-start | bytes 65536 | tf_op jit(solution)/shard_map/all_to_all | solution.py:20
  121.9 4.7 %all-to-all-done.1 = f32[8,2,512]{2,1,0:T(2,128)S(1)} async-done(((f32[8,2,512]{2,1,0:T(2,128)}), f32[8,2,512]{2,1,0:T(2,128)S(1)}, u32[]{:S(2)}, u32[]{:S(2)}) %all-to-all-start.1) | async-done | bytes 32800 | tf_op jit(solution)/shard_map/all_to_all | solution.py:20
  126.9 23.7 %while.31 = (s32[]{:T(128)}, f32[512,512]{1,0:T(8,128)}, bf16[4,512,512]{1,2,0:T(8,128)(2,1)S(1)}, f32[]{:T(128)}, bf16[4,512,512]{2,1,0:T(8,128)(2,1)}, /*index...) while((s32[]{:T(128)}, f32[512,512]{1,0:T(8,128)}, ...), condition=%wide.region_16.17_spmd.clone, body=%wide.region_15.16_spmd.clone.sunk | while | flops 539230208 | bytes 5253747 | solution.py:197
  126.9 2.5 bitcast_dynamic-update-slice_fusion.2
  129.4 3.1 %fusion.82 = f32[512,512]{1,0:T(8,128)} fusion(bf16[512,512]{1,0:T(8,128)(2,1)S(1)} %get-tuple-element.337, f32[512,512]{1,0:T(8,128)} %get-tuple-element.380, f32[]{:T(128)} %get-tuple-element.392, pred[]{:T(512)S(6)} %compare.7, bf16[4,512,512]{2,1,0:T(8,128)(2,1)} %get-tuple-element.393, s32[]{:T(128)} %get-tuple-element.379), kind=kOutput, calls=%fused_computation.10.clone.1 | convolution fusion | flops 269221888 | bytes 3146753 | tf_op jit(solution)/shard_map/while/body/eval_jaxpr/dot_general | solution.py:192
  132.6 2.5 bitcast_dynamic-update-slice_fusion.2
  135.1 3.5 %fusion.82 = f32[512,512]{1,0:T(8,128)} fusion(bf16[512,512]{1,0:T(8,128)(2,1)S(1)} %get-tuple-element.337, f32[512,512]{1,0:T(8,128)} %get-tuple-element.380, f32[]{:T(128)} %get-tuple-element.392, pred[]{:T(512)S(6)} %compare.7, bf16[4,512,512]{2,1,0:T(8,128)(2,1)} %get-tuple-element.393, s32[]{:T(128)} %get-tuple-element.379), kind=kOutput, calls=%fused_computation.10.clone.1 | convolution fusion | flops 269221888 | bytes 3146753 | tf_op jit(solution)/shard_map/while/body/eval_jaxpr/dot_general | solution.py:192
  138.6 2.5 bitcast_dynamic-update-slice_fusion.2
  141.1 3.5 %fusion.82 = f32[512,512]{1,0:T(8,128)} fusion(bf16[512,512]{1,0:T(8,128)(2,1)S(1)} %get-tuple-element.337, f32[512,512]{1,0:T(8,128)} %get-tuple-element.380, f32[]{:T(128)} %get-tuple-element.392, pred[]{:T(512)S(6)} %compare.7, bf16[4,512,512]{2,1,0:T(8,128)(2,1)} %get-tuple-element.393, s32[]{:T(128)} %get-tuple-element.379), kind=kOutput, calls=%fused_computation.10.clone.1 | convolution fusion | flops 269221888 | bytes 3146753 | tf_op jit(solution)/shard_map/while/body/eval_jaxpr/dot_general | solution.py:192
  144.6 2.5 bitcast_dynamic-update-slice_fusion.2
  147.1 3.5 %fusion.82 = f32[512,512]{1,0:T(8,128)} fusion(bf16[512,512]{1,0:T(8,128)(2,1)S(1)} %get-tuple-element.337, f32[512,512]{1,0:T(8,128)} %get-tuple-element.380, f32[]{:T(128)} %get-tuple-element.392, pred[]{:T(512)S(6)} %compare.7, bf16[4,512,512]{2,1,0:T(8,128)(2,1)} %get-tuple-element.393, s32[]{:T(128)} %get-tuple-element.379), kind=kOutput, calls=%fused_computation.10.clone.1 | convolution fusion | flops 269221888 | bytes 3146753 | tf_op jit(solution)/shard_map/while/body/eval_jaxpr/dot_general | solution.py:192
  150.6 4.2 %convolution_multiply_fusion.3 = f32[2048,512]{1,0:T(8,128)} fusion(bf16[2048,512]{1,0:T(8,128)(2,1)S(1)} %bitcast.243, bf16[512,512]{1,0:T(8,128)(2,1)} %bitcast.2, f32[]{:T(128)} %bitcast.241), kind=kOutput, calls=%fused_computation.21 | convolution fusion | flops 1074790400 | bytes 6815748 | tf_op jit(solution)/shard_map/dot_general | solution.py:200
  154.9 51.6 %reduce-scatter.3.cloned.1.call-done = f32[256,512]{1,0:T(8,128)} async-done(((f32[2048,512]{1,0:T(8,128)}), f32[256,512]{1,0:T(8,128)}) %reduce-scatter.3.cloned.1.call-update) | async-done | bytes 524304 | tf_op jit(solution)/shard_map/reduce_scatter | solution.py:97
  206.5 4.9 %all-to-all-start.2 = ((f32[8,64,512]{2,1,0:T(8,128)}), f32[8,64,512]{2,1,0:T(8,128)S(1)}, u32[]{:S(2)}, u32[]{:S(2)}) async-start(f32[8,64,512]{2,1,0:T(8,128)} %bitcast.35), calls=%async_computation.2 | async-start | bytes 2097152 | tf_op jit(solution)/shard_map/all_to_all | solution.py:109
  211.4 15.1 %all-to-all-done.2 = f32[8,64,512]{2,1,0:T(8,128)S(1)} async-done(((f32[8,64,512]{2,1,0:T(8,128)}), f32[8,64,512]{2,1,0:T(8,128)S(1)}, u32[]{:S(2)}, u32[]{:S(2)}) %all-to-all-start.2) | async-done | bytes 1048608 | tf_op jit(solution)/shard_map/all_to_all | solution.py:109
  226.5 0.1 reduce_sum.95
  226.6 3.4 %reduce-scatter.5.cloned.1.call-done = f32[64,512]{1,0:T(8,128)} async-done(((f32[256,512]{1,0:T(8,128)}), f32[64,512]{1,0:T(8,128)}) %reduce-scatter.5.cloned.1.call-update) | async-done | bytes 131088 | tf_op jit(solution)/shard_map/reduce_scatter | solution.py:97
  230.0 1.2 multiply_reduce_fusion
  231.2 0.7 subtract_reduce_fusion
  233.2 14.2 %psum.28 = f32[]{:T(128)} all-reduce(f32[]{:T(128)S(6)} %add.191), channel_id=1, replica_groups=mesh['row_0'=8,'row_1'=4,'col_0'=4,'col_1'=2] {'row_0'}, use_global_device_ids=true, to_apply=%region_11.12 | all-reduce | flops 1 | bytes 8 | tf_op jit(solution)/shard_map/psum | solution.py:91
  247.4 7.5 %psum.29 = f32[]{:T(128)} all-reduce(f32[]{:T(128)} %psum.28), channel_id=1, replica_groups=mesh['row_0'=8,'row_1'=4,'col_0'=4,'col_1'=2] {'row_1'}, use_global_device_ids=true, to_apply=%region_12.13 | all-reduce | flops 1 | bytes 8 | tf_op jit(solution)/shard_map/psum | solution.py:91
  254.9 9.0 %psum.30 = f32[]{:T(128)} all-reduce(f32[]{:T(128)} %psum.29), channel_id=1, replica_groups=mesh['row_0'=8,'row_1'=4,'col_0'=4,'col_1'=2] {'col_0'}, use_global_device_ids=true, to_apply=%region_13.14 | all-reduce | flops 1 | bytes 8 | tf_op jit(solution)/shard_map/psum | solution.py:91
  263.8 12.3 %psum.31 = f32[]{:T(128)} all-reduce(f32[]{:T(128)} %psum.30), channel_id=1, replica_groups=mesh['row_0'=8,'row_1'=4,'col_0'=4,'col_1'=2] {'col_1'}, use_global_device_ids=true, to_apply=%region_14.15 | all-reduce | flops 1 | bytes 8 | tf_op jit(solution)/shard_map/psum | solution.py:91
  276.8 1.7 subtract_divide_fusion
  (71 shorter events, 1.1 us)
Async XLA Ops:
  7.2 56.3 %all-gather.6.cloned.1.call-start = ((), (), s32[]{:S(2)}) async-start(), calls=%async_computation.5 | async-start | bytes 2359296 | tf_op jit(solution)/shard_map/all_gather | solution.py:29
  23.8 18.0 %all-to-all-start = ((bf16[8,64,512]{2,1,0:T(8,128)(2,1)}), bf16[8,64,512]{2,1,0:T(8,128)(2,1)}, u32[]{:S(2)}, u32[]{:S(2)}) async-start(bf16[8,64,512]{2,1,0:T(8,128)(2,1)} %broadcast_in_dim.39), calls=%async_computation | async-start | bytes 1048576 | tf_op jit(solution)/shard_map/all_to_all | solution.py:20
  104.3 22.2 %all-to-all-start.1 = ((f32[8,2,512]{2,1,0:T(2,128)}), f32[8,2,512]{2,1,0:T(2,128)S(1)}, u32[]{:S(2)}, u32[]{:S(2)}) async-start(f32[8,2,512]{2,1,0:T(2,128)} %broadcast_in_dim.40), calls=%async_computation.1 | async-start | bytes 65536 | tf_op jit(solution)/shard_map/all_to_all | solution.py:20
  121.8 84.7 %reduce-scatter.3.cloned.1.call-start = ((), (), s32[]{:S(2)}) async-start(), calls=%async_computation.6 | async-start | bytes 4718592 | tf_op jit(solution)/shard_map/reduce_scatter | solution.py:97
  154.8 75.1 %copy-start = (bf16[64,512]{1,0:T(8,128)(2,1)S(1)}, bf16[64,512]{1,0:T(8,128)(2,1)}, u32[]{:S(2)}) copy-start(bf16[64,512]{1,0:T(8,128)(2,1)} %param.8) | copy-start | bytes 196612
  154.8 75.1 %copy-start.1 = (bf16[64,512]{1,0:T(8,128)(2,1)S(1)}, bf16[64,512]{1,0:T(8,128)(2,1)}, u32[]{:S(2)}) copy-start(bf16[64,512]{1,0:T(8,128)(2,1)} %param.7) | copy-start | bytes 196612
  154.9 75.1 %reduce-scatter.5.cloned.1.call-start = ((), (), s32[]{:S(2)}) async-start(), calls=%async_computation.7 | async-start | bytes 655360 | tf_op jit(solution)/shard_map/reduce_scatter | solution.py:97
  206.5 20.0 %all-to-all-start.2 = ((f32[8,64,512]{2,1,0:T(8,128)}), f32[8,64,512]{2,1,0:T(8,128)S(1)}, u32[]{:S(2)}, u32[]{:S(2)}) async-start(f32[8,64,512]{2,1,0:T(8,128)} %bitcast.35), calls=%async_computation.2 | async-start | bytes 2097152 | tf_op jit(solution)/shard_map/all_to_all | solution.py:109
Sparse Core Ops, SparseCore 0:
  21.2 42.2 all-gather.5
  155.0 51.5 reduce-scatter.2
  209.1 20.8 reduce-scatter.4
where the time goes:
time: 287 us; the launch traced here: 286 us
  waiting for transfers between devices  105 us (37%)
  blocking collectives  82.8 us (29%)
  matrix products  37.4 us (13%)
  starting transfers between devices  30.8 us (11%)
  between operations  17.6 us (6%)
  other arithmetic  9.43 us (3%)
    reduce_scatter x2, waiting for transfers between devices, sum_by_axis(): total = lax.psum_scatter(total, axis, scatter_dimension=0, tiled=True)  55 us
    psum x4, blocking collectives, over_axes(): value = lax.psum(value, axis)  43 us
    all_gather x2, blocking collectives, all_in_one_2(): both, at, found = (lax.all_gather(jnp.concatenate(lines), axis), 0, {})  27.9 us
    all_to_all x2, starting transfers between devices, from_everyone(): return lax.all_to_all(copies, axis, split_axis=0, concat_axis=0, tiled=True)  25.9 us
    all_gather x1, waiting for transfers between devices, gather_axes(): value = lax.all_gather(value, axis, axis=dim, tiled=True)  21.7 us
    dot_general x8, matrix products, scores(): jnp.einsum('re,ce->rc', img_tile, txt_block, preferred_element_type=jnp.f...  19.6 us
    all_to_all x1, waiting for transfers between devices, summed_on_arrival(): tiles = lax.all_to_all(in_blocks(value, dim, count), axis, 0, 0, tiled=True)  15.1 us
    all_to_all x2, waiting for transfers between devices, from_everyone(): return lax.all_to_all(copies, axis, split_axis=0, concat_axis=0, tiled=True)  13.6 us
  transfers between devices with their start and end apart: 6, of which 6 were waited for; matrix products, arithmetic and copies ran while one was open for 1% of the time, Pallas kernels for 0%

commit v1 on v0

--- a/solution.py
+++ b/solution.py
@@ -88,7 +88,7 @@
 
 def over_axes(value, axes):
     for axis in axes:
-        value = lax.psum(value, axis)
+        value = jnp.sum(lax.all_gather(value, axis), axis=0)
     return value
 
 

time: 287 us -> 295 us (1.028)
  local copies, waits for them, and re-layouts: 2.4 us -> 9.72 us
  other arithmetic: 9.43 us -> 12.5 us
    psum x4 -> x0, blocking collectives: 43 us -> none  [over_axes(): value = lax.psum(value, axis)]
    unnamed x0 -> x4, blocking collectives: none -> 40.6 us
    unnamed x8 -> x26, local copies, waits for them, and re-layouts: 0.04 us -> 7.36 us
where the time goes in v1:
time: 295 us; the launch traced here: 294 us
  waiting for transfers between devices  105 us (36%)
  blocking collectives  80.4 us (27%)
  matrix products  37.4 us (13%)
  starting transfers between devices  31 us (11%)
  between operations  17.7 us (6%)
  other arithmetic  12.5 us (4%)
  local copies, waits for them, and re-layouts  9.72 us (3%)
    reduce_scatter x2, waiting for transfers between devices, sum_by_axis(): total = lax.psum_scatter(total, axis, scatter_dimension=0, tiled=True)  54.8 us
    unnamed x4, blocking collectives  40.6 us
    all_gather x2, blocking collectives, all_in_one_2(): both, at, found = (lax.all_gather(jnp.concatenate(lines), axis), 0, {})  27.9 us
    all_to_all x2, starting transfers between devices, from_everyone(): return lax.all_to_all(copies, axis, split_axis=0, concat_axis=0, tiled=True)  25.9 us
    all_gather x1, waiting for transfers between devices, gather_axes(): value = lax.all_gather(value, axis, axis=dim, tiled=True)  21.7 us
    dot_general x8, matrix products, scores(): jnp.einsum('re,ce->rc', img_tile, txt_block, preferred_element_type=jnp.f...  19.6 us
    all_to_all x1, waiting for transfers between devices, summed_on_arrival(): tiles = lax.all_to_all(in_blocks(value, dim, count), axis, 0, 0, tiled=True)  14.5 us
    all_to_all x2, waiting for transfers between devices, from_everyone(): return lax.all_to_all(copies, axis, split_axis=0, concat_axis=0, tiled=True)  13.6 us
  transfers between devices with their start and end apart: 6, of which 6 were waited for; matrix products, arithmetic and copies ran while one was open for 1% of the time, Pallas kernels for 0%

profile of v1, /device:TPU:1, one launch (start us, length us, event | category | flops | bytes accessed | tf_op | source)
XLA Modules:
  0.0 293.7 jit_solution(2715387670934187402)
XLA Ops:
  7.2 1.0 fusion.11
  8.2 0.9 fusion.58
  9.1 11.9 %all_gather.42 = bf16[256,512]{1,0:T(8,128)(2,1)} all-gather(bf16[64,512]{1,0:T(8,128)(2,1)S(1)} %fusion.58), channel_id=1, replica_groups=mesh['row_0'=8,'row_1'=4,'col_0'=4,'col_1'=2] {'row_1'}, dimensions={0}, use_global_device_ids=true | all-gather | bytes 327680 | tf_op jit(solution)/shard_map/all_gather | solution.py:29
  21.1 1.0 fusion.12
  22.0 0.9 fusion.59
  23.0 0.8 broadcast_in_dim.39
  23.8 8.4 %all-to-all-start = ((bf16[8,64,512]{2,1,0:T(8,128)(2,1)}), bf16[8,64,512]{2,1,0:T(8,128)(2,1)}, u32[]{:S(2)}, u32[]{:S(2)}) async-start(bf16[8,64,512]{2,1,0:T(8,128)(2,1)} %broadcast_in_dim.39), calls=%async_computation | async-start | bytes 1048576 | tf_op jit(solution)/shard_map/all_to_all | solution.py:20
  32.8 8.9 %all-to-all-done = bf16[8,64,512]{2,1,0:T(8,128)(2,1)} async-done(((bf16[8,64,512]{2,1,0:T(8,128)(2,1)}), bf16[8,64,512]{2,1,0:T(8,128)(2,1)}, u32[]{:S(2)}, u32[]{:S(2)}) %all-to-all-start) | async-done | bytes 524320 | tf_op jit(solution)/shard_map/all_to_all | solution.py:20
  41.8 21.7 %all-gather.6.cloned.1.call-done = bf16[2048,512]{1,0:T(8,128)(2,1)} async-done(((bf16[256,512]{1,0:T(8,128)(2,1)}), bf16[2048,512]{1,0:T(8,128)(2,1)}) %all-gather.6.cloned.1.call-update) | async-done | bytes 2097168 | tf_op jit(solution)/shard_map/all_gather | solution.py:29
  63.5 11.7 %while.30 = (s32[]{:T(128)}, f32[512]{0:T(512)S(1)}, f32[512]{0:T(512)S(1)}, f32[4,512]{1,0:T(4,128)S(1)}, f32[4,512]{1,0:T(4,128)S(1)}, /*index=5*/f32[]{:T(128...) while((s32[]{:T(128)}, f32[512]{0:T(512)S(1)}, ...), condition=%wide.region_7.8_spmd.clone, body=%wide.region_2.7_spmd.clone.sunk | while | flops 270272000 | bytes 3187832 | solution.py:162
  63.5 2.4 fusion.77
  66.4 2.4 fusion.77
  69.4 2.4 fusion.77
  72.3 2.4 fusion.77
  75.3 18.5 %all-gather.2 = f32[8,2,2048]{2,1,0:T(2,128)S(1)} all-gather(f32[1,2,2048]{2,1,0:T(2,128)S(1)} %maximum_bitcast_fusion), channel_id=2, replica_groups=mesh['row_0'=8,'row_1'=4,'col_0'=4,'col_1'=2] {'row_0'}, dimensions={0}, use_global_device_ids=true | all-gather | bytes 147456 | tf_op jit(solution)/shard_map/all_gather | solution.py:71
  94.0 9.4 %all-gather.3 = f32[4,2,2048]{2,1,0:T(2,128)S(1)} all-gather(f32[1,2,2048]{2,1,0:T(2,128)S(1)} %maximum_bitcast_fusion.1), channel_id=3, replica_groups=mesh['row_0'=8,'row_1'=4,'col_0'=4,'col_1'=2] {'row_1'}, dimensions={0}, use_global_device_ids=true | all-gather | bytes 81920 | tf_op jit(solution)/shard_map/all_gather | solution.py:71
  103.7 0.6 broadcast_in_dim.40
  104.3 17.5 %all-to-all-start.1 = ((f32[8,2,512]{2,1,0:T(2,128)}), f32[8,2,512]{2,1,0:T(2,128)S(1)}, u32[]{:S(2)}, u32[]{:S(2)}) async-start(f32[8,2,512]{2,1,0:T(2,128)} %broadcast_in_dim.40), calls=%async_computation.1 | async-start | bytes 65536 | tf_op jit(solution)/shard_map/all_to_all | solution.py:20
  121.9 4.7 %all-to-all-done.1 = f32[8,2,512]{2,1,0:T(2,128)S(1)} async-done(((f32[8,2,512]{2,1,0:T(2,128)}), f32[8,2,512]{2,1,0:T(2,128)S(1)}, u32[]{:S(2)}, u32[]{:S(2)}) %all-to-all-start.1) | async-done | bytes 32800 | tf_op jit(solution)/shard_map/all_to_all | solution.py:20
  126.9 23.7 %while.31 = (s32[]{:T(128)}, f32[512,512]{1,0:T(8,128)}, bf16[4,512,512]{1,2,0:T(8,128)(2,1)S(1)}, f32[]{:T(128)}, bf16[4,512,512]{2,1,0:T(8,128)(2,1)}, /*index...) while((s32[]{:T(128)}, f32[512,512]{1,0:T(8,128)}, ...), condition=%wide.region_16.17_spmd.clone, body=%wide.region_15.16_spmd.clone.sunk | while | flops 539230208 | bytes 5253747 | solution.py:197
  126.9 2.5 bitcast_dynamic-update-slice_fusion.2
  129.4 3.1 %fusion.82 = f32[512,512]{1,0:T(8,128)} fusion(bf16[512,512]{1,0:T(8,128)(2,1)S(1)} %get-tuple-element.337, f32[512,512]{1,0:T(8,128)} %get-tuple-element.380, f32[]{:T(128)} %get-tuple-element.392, pred[]{:T(512)S(6)} %compare.7, bf16[4,512,512]{2,1,0:T(8,128)(2,1)} %get-tuple-element.393, s32[]{:T(128)} %get-tuple-element.379), kind=kOutput, calls=%fused_computation.10.clone.1 | convolution fusion | flops 269221888 | bytes 3146753 | tf_op jit(solution)/shard_map/while/body/eval_jaxpr/dot_general | solution.py:192
  132.6 2.5 bitcast_dynamic-update-slice_fusion.2
  135.1 3.5 %fusion.82 = f32[512,512]{1,0:T(8,128)} fusion(bf16[512,512]{1,0:T(8,128)(2,1)S(1)} %get-tuple-element.337, f32[512,512]{1,0:T(8,128)} %get-tuple-element.380, f32[]{:T(128)} %get-tuple-element.392, pred[]{:T(512)S(6)} %compare.7, bf16[4,512,512]{2,1,0:T(8,128)(2,1)} %get-tuple-element.393, s32[]{:T(128)} %get-tuple-element.379), kind=kOutput, calls=%fused_computation.10.clone.1 | convolution fusion | flops 269221888 | bytes 3146753 | tf_op jit(solution)/shard_map/while/body/eval_jaxpr/dot_general | solution.py:192
  138.6 2.5 bitcast_dynamic-update-slice_fusion.2
  141.1 3.5 %fusion.82 = f32[512,512]{1,0:T(8,128)} fusion(bf16[512,512]{1,0:T(8,128)(2,1)S(1)} %get-tuple-element.337, f32[512,512]{1,0:T(8,128)} %get-tuple-element.380, f32[]{:T(128)} %get-tuple-element.392, pred[]{:T(512)S(6)} %compare.7, bf16[4,512,512]{2,1,0:T(8,128)(2,1)} %get-tuple-element.393, s32[]{:T(128)} %get-tuple-element.379), kind=kOutput, calls=%fused_computation.10.clone.1 | convolution fusion | flops 269221888 | bytes 3146753 | tf_op jit(solution)/shard_map/while/body/eval_jaxpr/dot_general | solution.py:192
  144.6 2.5 bitcast_dynamic-update-slice_fusion.2
  147.1 3.5 %fusion.82 = f32[512,512]{1,0:T(8,128)} fusion(bf16[512,512]{1,0:T(8,128)(2,1)S(1)} %get-tuple-element.337, f32[512,512]{1,0:T(8,128)} %get-tuple-element.380, f32[]{:T(128)} %get-tuple-element.392, pred[]{:T(512)S(6)} %compare.7, bf16[4,512,512]{2,1,0:T(8,128)(2,1)} %get-tuple-element.393, s32[]{:T(128)} %get-tuple-element.379), kind=kOutput, calls=%fused_computation.10.clone.1 | convolution fusion | flops 269221888 | bytes 3146753 | tf_op jit(solution)/shard_map/while/body/eval_jaxpr/dot_general | solution.py:192
  150.6 4.2 %convolution_multiply_fusion.3 = f32[2048,512]{1,0:T(8,128)} fusion(bf16[2048,512]{1,0:T(8,128)(2,1)S(1)} %bitcast.250, bf16[512,512]{1,0:T(8,128)(2,1)} %bitcast.2, f32[]{:T(128)} %bitcast.247), kind=kOutput, calls=%fused_computation.21 | convolution fusion | flops 1074790400 | bytes 6815748 | tf_op jit(solution)/shard_map/dot_general | solution.py:200
  154.9 51.6 %reduce-scatter.3.cloned.1.call-done = f32[256,512]{1,0:T(8,128)} async-done(((f32[2048,512]{1,0:T(8,128)}), f32[256,512]{1,0:T(8,128)}) %reduce-scatter.3.cloned.1.call-update) | async-done | bytes 524304 | tf_op jit(solution)/shard_map/reduce_scatter | solution.py:97
  206.6 5.0 %all-to-all-start.2 = ((f32[8,64,512]{2,1,0:T(8,128)}), f32[8,64,512]{2,1,0:T(8,128)S(1)}, u32[]{:S(2)}, u32[]{:S(2)}) async-start(f32[8,64,512]{2,1,0:T(8,128)} %bitcast.43), calls=%async_computation.2 | async-start | bytes 2097152 | tf_op jit(solution)/shard_map/all_to_all | solution.py:109
  212.2 14.5 %all-to-all-done.2 = f32[8,64,512]{2,1,0:T(8,128)S(1)} async-done(((f32[8,64,512]{2,1,0:T(8,128)}), f32[8,64,512]{2,1,0:T(8,128)S(1)}, u32[]{:S(2)}, u32[]{:S(2)}) %all-to-all-start.2) | async-done | bytes 1048608 | tf_op jit(solution)/shard_map/all_to_all | solution.py:109
  226.8 3.2 %reduce-scatter.5.cloned.1.call-done = f32[64,512]{1,0:T(8,128)} async-done(((f32[256,512]{1,0:T(8,128)}), f32[64,512]{1,0:T(8,128)}) %reduce-scatter.5.cloned.1.call-update) | async-done | bytes 131088 | tf_op jit(solution)/shard_map/reduce_scatter | solution.py:97
  230.0 1.2 multiply_reduce_fusion
  231.2 0.7 subtract_reduce_fusion
  233.2 0.8 dynamic-update-slice
  234.5 13.7 %all-reduce = f32[8]{0:T(128)S(1)} all-reduce(f32[8]{0:T(128)S(1)} %dynamic-update-slice), channel_id=1, replica_groups=mesh['row_0'=8,'row_1'=4,'col_0'=4,'col_1'=2] {'row_0'}, use_global_device_ids=true, to_apply=%add | all-reduce | flops 8 | bytes 64
  248.2 0.6 reduce_sum.131
  248.8 1.4 dynamic-update-slice.1
  250.8 6.8 %all-reduce.1 = f32[4]{0:T(128)S(1)} all-reduce(f32[4]{0:T(128)S(1)} %dynamic-update-slice.1), channel_id=1, replica_groups=mesh['row_0'=8,'row_1'=4,'col_0'=4,'col_1'=2] {'row_1'}, use_global_device_ids=true, to_apply=%add.1 | all-reduce | flops 4 | bytes 32
  257.6 0.6 reduce_sum.132
  258.2 1.4 dynamic-update-slice.2
  260.2 8.1 %all-reduce.2 = f32[4]{0:T(128)S(1)} all-reduce(f32[4]{0:T(128)S(1)} %dynamic-update-slice.2), channel_id=1, replica_groups=mesh['row_0'=8,'row_1'=4,'col_0'=4,'col_1'=2] {'col_0'}, use_global_device_ids=true, to_apply=%add.2 | all-reduce | flops 4 | bytes 32
  268.3 0.6 reduce_sum.133
  268.9 1.4 dynamic-update-slice.3
  270.3 12.1 %all-reduce.3 = f32[2]{0:T(128)S(1)} all-reduce(f32[2]{0:T(128)S(1)} %dynamic-update-slice.3), channel_id=1, replica_groups=mesh['row_0'=8,'row_1'=4,'col_0'=4,'col_1'=2] {'col_1'}, use_global_device_ids=true, to_apply=%add.3 | all-reduce | flops 2 | bytes 16
  282.4 0.8 subtract_divide_fusion.1
  284.4 1.7 subtract_divide_fusion
  (95 shorter events, 6.1 us)
Async XLA Ops:
  7.2 56.3 %all-gather.6.cloned.1.call-start = ((), (), s32[]{:S(2)}) async-start(), calls=%async_computation.5 | async-start | bytes 2359296 | tf_op jit(solution)/shard_map/all_gather | solution.py:29
  23.8 18.0 %all-to-all-start = ((bf16[8,64,512]{2,1,0:T(8,128)(2,1)}), bf16[8,64,512]{2,1,0:T(8,128)(2,1)}, u32[]{:S(2)}, u32[]{:S(2)}) async-start(bf16[8,64,512]{2,1,0:T(8,128)(2,1)} %broadcast_in_dim.39), calls=%async_computation | async-start | bytes 1048576 | tf_op jit(solution)/shard_map/all_to_all | solution.py:20
  104.3 22.2 %all-to-all-start.1 = ((f32[8,2,512]{2,1,0:T(2,128)}), f32[8,2,512]{2,1,0:T(2,128)S(1)}, u32[]{:S(2)}, u32[]{:S(2)}) async-start(f32[8,2,512]{2,1,0:T(2,128)} %broadcast_in_dim.40), calls=%async_computation.1 | async-start | bytes 65536 | tf_op jit(solution)/shard_map/all_to_all | solution.py:20
  121.8 84.7 %reduce-scatter.3.cloned.1.call-start = ((), (), s32[]{:S(2)}) async-start(), calls=%async_computation.6 | async-start | bytes 4718592 | tf_op jit(solution)/shard_map/reduce_scatter | solution.py:97
  154.8 56.8 %copy-start.5 = (u32[256]{0:T(256)S(1)}, u32[256]{0:T(256)}, u32[]{:S(2)}) copy-start(u32[256]{0:T(256)} %constant.73) | copy-start | bytes 3076
  154.8 75.2 %copy-start = (bf16[64,512]{1,0:T(8,128)(2,1)S(1)}, bf16[64,512]{1,0:T(8,128)(2,1)}, u32[]{:S(2)}) copy-start(bf16[64,512]{1,0:T(8,128)(2,1)} %param.8) | copy-start | bytes 196612
  154.9 75.2 %copy-start.1 = (bf16[64,512]{1,0:T(8,128)(2,1)S(1)}, bf16[64,512]{1,0:T(8,128)(2,1)}, u32[]{:S(2)}) copy-start(bf16[64,512]{1,0:T(8,128)(2,1)} %param.7) | copy-start | bytes 196612
  154.9 75.1 %reduce-scatter.5.cloned.1.call-start = ((), (), s32[]{:S(2)}) async-start(), calls=%async_computation.7 | async-start | bytes 655360 | tf_op jit(solution)/shard_map/reduce_scatter | solution.py:97
  206.5 27.4 %copy-start.4 = (u32[256]{0:T(256)S(1)}, u32[256]{0:T(256)}, u32[]{:S(2)}) copy-start(u32[256]{0:T(256)} %constant.78) | copy-start | bytes 3076
  206.5 43.7 %copy-start.3 = (u32[256]{0:T(256)S(1)}, u32[256]{0:T(256)}, u32[]{:S(2)}) copy-start(u32[256]{0:T(256)} %constant.83) | copy-start | bytes 3076
  206.6 53.1 %copy-start.2 = (u32[256]{0:T(256)S(1)}, u32[256]{0:T(256)}, u32[]{:S(2)}) copy-start(u32[256]{0:T(256)} %constant.88) | copy-start | bytes 3076
  206.6 20.1 %all-to-all-start.2 = ((f32[8,64,512]{2,1,0:T(8,128)}), f32[8,64,512]{2,1,0:T(8,128)S(1)}, u32[]{:S(2)}, u32[]{:S(2)}) async-start(f32[8,64,512]{2,1,0:T(8,128)} %bitcast.43), calls=%async_computation.2 | async-start | bytes 2097152 | tf_op jit(solution)/shard_map/all_to_all | solution.py:109
Sparse Core Ops, SparseCore 0:
  21.2 42.2 all-gather.5
  154.9 51.5 reduce-scatter.2
  209.0 20.9 reduce-scatter.4
